TPU v7x, 512 devices: a whole 4x4x16 slice. The times are simulated.
512 devices in a mesh: tok: 16 (over z), col: 32 (over x, y, core).
Axes of the slice: x: 4, y: 4, z: 16, core: 2. Of those that a mesh axis runs over, the one named last changes fastest.
Arguments:
- acts: bfloat16 [8192, 28672], P('tok', 'col'), may hold values from -6 to 6
- residual: float32 [8192, 8192], P('tok', 'col'), may hold values from -6 to 6
- weights: bfloat16 [32, 896, 8192], P(None, 'tok', 'col'), may hold values from -6 to 6
- order: int32 [4], replicated, may hold values from 0 to 31
- rate: float32 [32], replicated, may hold values from 0.1 to 0.4
- penalty: float32 [32], replicated, may hold values from 0.4 to 1.2
Outputs:
- pruned: float32 [32, 896, 8192], P(None, 'tok', 'col')
- resid_out: float32 [8192, 8192], P('tok', 'col')
Inputs may be any that keep to these rules, and one draw needn't show every extreme that they name: `order`: block indices, repeats allowed.
All inputs are finite; a program needn't handle non-finite values.
Results may differ from a plain program's by a relative error of at most 0.0054.
Values may be sent and summed in bfloat16 or wider, within the bound.
A program may use at most 64 MiB of HBM per device.

v0:
```python
import math
import jax
import jax.numpy as jnp
from jax import lax
from jax.sharding import PartitionSpec as P

D = 8192
CH = 28672
STEPS = 4


def from_root(block, axis, holder):
    block = jnp.where(lax.axis_index(axis) == holder, block, jnp.zeros_like(block))
    return lax.psum(block, axis)


def body(acts, residual, weights, order, rate, penalty):
    tok_rows = acts.shape[0]
    scale = math.sqrt(CH)
    thresh_unit = math.sqrt(D)
    eta_unit = float(CH) / float(tok_rows * lax.axis_size("tok"))
    state = weights.astype(jnp.float32)
    resid = residual
    for step in range(STEPS):
        which = order[step]
        block_acts = from_root(acts, "col", which)
        lowered = resid.astype(jnp.bfloat16)
        partial_grad = lax.dot_general(
            block_acts, lowered, (((0,), (0,)), ((), ())), preferred_element_type=jnp.float32
        )
        current = lax.dynamic_index_in_dim(state, which, 0, keepdims=False)
        step_size = rate[which] * eta_unit
        limit = penalty[which] * thresh_unit
        grad = lax.psum_scatter(partial_grad, "tok", scatter_dimension=0, tiled=True) / scale
        shifted = current - step_size * grad
        sums = lax.psum(jnp.sum(shifted * shifted, axis=1), "col")
        factor = jnp.maximum(0.0, 1.0 - limit / jnp.sqrt(sums + 1e-06))
        fresh = factor[:, None] * shifted
        local_change = (fresh - current).astype(jnp.bfloat16)
        state = lax.dynamic_update_index_in_dim(state, fresh, which, 0)
        change = lax.all_gather(local_change, "tok", axis=0, tiled=True)
        resid = resid + jnp.dot(block_acts, change, preferred_element_type=jnp.float32) / scale
    return (state, resid)


def solution(mesh):
    in_specs = (P("tok", "col"), P("tok", "col"), P(None, "tok", "col"), P(), P(), P())
    out_specs = (P(None, "tok", "col"), P("tok", "col"))
    return jax.shard_map(body, mesh=mesh, in_specs=in_specs, out_specs=out_specs, check_vma=False)
```

profile of v0, /device:TPU:32, one launch (start us, length us, event | category | flops | bytes accessed | tf_op | source)
XLA Modules:
  0.0 816.7 jit_solution(8121737015502011051)
XLA Ops:
  7.2 0.0 all-reduce.3.cloned.1.call-start
  7.2 1.4 fusion.18
  11.1 3.1 broadcast_select_fusion
  14.2 0.0 all-reduce.3.cloned.1.call-update
  14.3 0.0 reduce-scatter.5.cloned.1.call-start
  14.3 145.9 %all-reduce.3.cloned.1.call-done = (bf16[512,896]{1,0:T(8,128)(2,1)}, bf16[512,896]{1,0:T(8,128)(2,1)}, bf16[512,896]{1,0:T(8,128)(2,1)}, bf16[512,896]{1,0:T(8,128)(2,1)}) async-done(((bf16[512,896]{1,0:T(8,128)(2,1)}, bf16[512,896]{1,0:T(8,128)(2,1)}, bf16[512,896]{1,0:T(8,128)(2,1)}, bf16[512,896]{1,0:T(8,128)(2,1)}), (bf16[512,896]{1,0:T(8,128)(2,1)}, bf16[512,896]{1,0:T(8,128)(2,1)}, ...) | async-done | bytes 3670032 | tf_op jit(solution)/shard_map/psum | solution.py:14
  160.2 2.5 fusion.10
  162.7 0.0 reduce-scatter.5.cloned.1.call-update
  162.8 0.0 reduce-scatter.7.cloned.1.call-start
  167.8 1.4 convert_element_type.27
  171.7 0.7 fusion.17
  173.0 0.7 fusion.16
  174.4 57.9 %reduce-scatter.5.cloned.1.call-done = f32[56,256]{1,0:T(8,128)} async-done(((f32[896,256]{1,0:T(8,128)}), f32[56,256]{1,0:T(8,128)}) %reduce-scatter.5.cloned.1.call-update) | async-done | bytes 57360 | tf_op jit(solution)/shard_map/reduce_scatter | solution.py:34
  232.3 1.0 multiply_reduce_fusion.3
  233.2 62.7 %psum.57 = f32[56]{0:T(128)S(1)} all-reduce(f32[56]{0:T(128)S(1)} %get-tuple-element.12), channel_id=1, replica_groups=mesh['tok'=16,'col'=32] {'col'}, use_global_device_ids=true, to_apply=%region_3.4 | all-reduce | flops 56 | bytes 448 | tf_op jit(solution)/shard_map/psum | solution.py:36
  295.9 0.9 fusion.15
  296.8 29.3 %all_gather.12 = bf16[896,256]{1,0:T(8,128)(2,1)S(1)} all-gather(bf16[56,256]{1,0:T(8,128)(2,1)S(1)} %fusion.15), channel_id=1, replica_groups=mesh['tok'=16,'col'=32] {'tok'}, dimensions={0}, use_global_device_ids=true | all-gather | bytes 487424 | tf_op jit(solution)/shard_map/all_gather | solution.py:41
  326.2 0.4 fusion
  326.6 1.4 fusion.8
  328.0 0.0 reduce-scatter.7.cloned.1.call-update
  328.0 0.0 reduce-scatter.9.cloned.1.call-start
  329.3 0.7 bitcast_dynamic-update-slice_fusion.3
  330.0 62.9 %reduce-scatter.7.cloned.1.call-done = f32[56,256]{1,0:T(8,128)} async-done(((f32[896,256]{1,0:T(8,128)}), f32[56,256]{1,0:T(8,128)}) %reduce-scatter.7.cloned.1.call-update) | async-done | bytes 57360 | tf_op jit(solution)/shard_map/reduce_scatter | solution.py:34
  392.9 1.0 multiply_reduce_fusion.2
  393.8 62.7 %psum.59 = f32[56]{0:T(128)S(1)} all-reduce(f32[56]{0:T(128)S(1)} %get-tuple-element.10), channel_id=1, replica_groups=mesh['tok'=16,'col'=32] {'col'}, use_global_device_ids=true, to_apply=%region_7.8 | all-reduce | flops 56 | bytes 448 | tf_op jit(solution)/shard_map/psum | solution.py:36
  456.5 0.9 fusion.14
  457.4 29.4 %all_gather.13 = bf16[896,256]{1,0:T(8,128)(2,1)S(1)} all-gather(bf16[56,256]{1,0:T(8,128)(2,1)S(1)} %fusion.14), channel_id=1, replica_groups=mesh['tok'=16,'col'=32] {'tok'}, dimensions={0}, use_global_device_ids=true | all-gather | bytes 487424 | tf_op jit(solution)/shard_map/all_gather | solution.py:41
  486.9 0.4 fusion.1
  487.3 1.4 fusion.6
  488.7 0.0 reduce-scatter.9.cloned.1.call-update
  488.8 0.0 reduce-scatter.11.cloned.1.call-start
  490.2 0.7 bitcast_dynamic-update-slice_fusion.2
  490.9 62.7 %reduce-scatter.9.cloned.1.call-done = f32[56,256]{1,0:T(8,128)} async-done(((f32[896,256]{1,0:T(8,128)}), f32[56,256]{1,0:T(8,128)}) %reduce-scatter.9.cloned.1.call-update) | async-done | bytes 57360 | tf_op jit(solution)/shard_map/reduce_scatter | solution.py:34
  553.6 1.0 multiply_reduce_fusion.1
  554.5 62.7 %psum.61 = f32[56]{0:T(128)S(1)} all-reduce(f32[56]{0:T(128)S(1)} %get-tuple-element.8), channel_id=1, replica_groups=mesh['tok'=16,'col'=32] {'col'}, use_global_device_ids=true, to_apply=%region_11.12 | all-reduce | flops 56 | bytes 448 | tf_op jit(solution)/shard_map/psum | solution.py:36
  617.2 0.9 fusion.13
  618.1 29.4 %all_gather.14 = bf16[896,256]{1,0:T(8,128)(2,1)S(1)} all-gather(bf16[56,256]{1,0:T(8,128)(2,1)S(1)} %fusion.13), channel_id=1, replica_groups=mesh['tok'=16,'col'=32] {'tok'}, dimensions={0}, use_global_device_ids=true | all-gather | bytes 487424 | tf_op jit(solution)/shard_map/all_gather | solution.py:41
  647.6 0.4 fusion.2
  648.0 1.4 fusion.4
  649.4 0.0 reduce-scatter.11.cloned.1.call-update
  650.7 0.7 bitcast_dynamic-update-slice_fusion.1
  651.4 62.8 %reduce-scatter.11.cloned.1.call-done = f32[56,256]{1,0:T(8,128)} async-done(((f32[896,256]{1,0:T(8,128)}), f32[56,256]{1,0:T(8,128)}) %reduce-scatter.11.cloned.1.call-update) | async-done | bytes 57360 | tf_op jit(solution)/shard_map/reduce_scatter | solution.py:34
  714.2 1.0 multiply_reduce_fusion
  715.2 62.7 %psum.63 = f32[56]{0:T(128)S(1)} all-reduce(f32[56]{0:T(128)S(1)} %get-tuple-element.6), channel_id=1, replica_groups=mesh['tok'=16,'col'=32] {'col'}, use_global_device_ids=true, to_apply=%region_15.16 | all-reduce | flops 56 | bytes 448 | tf_op jit(solution)/shard_map/psum | solution.py:36
  777.9 0.9 fusion.12
  778.8 0.7 bitcast_dynamic-update-slice_fusion
  779.5 29.4 %all_gather.15 = bf16[896,256]{1,0:T(8,128)(2,1)S(1)} all-gather(bf16[56,256]{1,0:T(8,128)(2,1)S(1)} %fusion.12), channel_id=1, replica_groups=mesh['tok'=16,'col'=32] {'tok'}, dimensions={0}, use_global_device_ids=true | all-gather | bytes 487424 | tf_op jit(solution)/shard_map/all_gather | solution.py:41
  808.9 1.2 fusion.3
  (20 shorter events, 0.1 us)
Async XLA Ops:
  7.2 153.0 %all-reduce.3.cloned.1.call-start = ((), (), s32[]{:S(2)}) async-start(), calls=%async_computation.8 | async-start | bytes 7340032 | tf_op jit(solution)/shard_map/psum | solution.py:14
  14.2 146.0 %copy-start.4 = (f32[512,256]{1,0:T(8,128)S(1)}, f32[512,256]{1,0:T(8,128)}, u32[]{:S(2)}) copy-start(f32[512,256]{1,0:T(8,128)} %param.7) | copy-start | bytes 1572868
  14.2 153.5 %copy-start.5 = (bf16[32,56,256]{2,1,0:T(8,128)(2,1)S(1)}, bf16[32,56,256]{2,1,0:T(8,128)(2,1)}, u32[]{:S(2)}) copy-start(bf16[32,56,256]{2,1,0:T(8,128)(2,1)} %param.8) | copy-start | bytes 2752516
  14.3 218.0 %reduce-scatter.5.cloned.1.call-start = ((), (), s32[]{:S(2)}) async-start(), calls=%async_computation.4 | async-start | bytes 974848 | tf_op jit(solution)/shard_map/reduce_scatter | solution.py:34
  162.7 9.0 %copy-start.6 = (f32[32]{0:T(128)S(1)}, f32[32]{0:T(128)}, u32[]{:S(2)}) copy-start(f32[32]{0:T(128)} %param.10) | copy-start | bytes 388
  162.7 10.3 %copy-start.7 = (f32[32]{0:T(128)S(1)}, f32[32]{0:T(128)}, u32[]{:S(2)}) copy-start(f32[32]{0:T(128)} %param.11) | copy-start | bytes 388
  162.7 163.4 %copy-start.3 = (bf16[512,896]{1,0:T(8,128)(2,1)S(1)}, bf16[512,896]{1,0:T(8,128)(2,1)}, u32[]{:S(2)}) copy-start(bf16[512,896]{1,0:T(8,128)(2,1)} %get-tuple-element.2) | copy-start | bytes 2752516
  162.8 230.1 %reduce-scatter.7.cloned.1.call-start = ((), (), s32[]{:S(2)}) async-start(), calls=%async_computation.5 | async-start | bytes 974848 | tf_op jit(solution)/shard_map/reduce_scatter | solution.py:34
  169.2 157.5 %copy-start.2 = (bf16[512,896]{1,0:T(8,128)(2,1)S(1)}, bf16[512,896]{1,0:T(8,128)(2,1)}, u32[]{:S(2)}) copy-start(bf16[512,896]{1,0:T(8,128)(2,1)} %get-tuple-element.3) | copy-start | bytes 2752516
  328.0 159.3 %copy-start.1 = (bf16[512,896]{1,0:T(8,128)(2,1)S(1)}, bf16[512,896]{1,0:T(8,128)(2,1)}, u32[]{:S(2)}) copy-start(bf16[512,896]{1,0:T(8,128)(2,1)} %get-tuple-element.4) | copy-start | bytes 2752516
  328.0 225.6 %reduce-scatter.9.cloned.1.call-start = ((), (), s32[]{:S(2)}) async-start(), calls=%async_computation.6 | async-start | bytes 974848 | tf_op jit(solution)/shard_map/reduce_scatter | solution.py:34
  488.8 159.3 %copy-start = (bf16[512,896]{1,0:T(8,128)(2,1)S(1)}, bf16[512,896]{1,0:T(8,128)(2,1)}, u32[]{:S(2)}) copy-start(bf16[512,896]{1,0:T(8,128)(2,1)} %get-tuple-element.5) | copy-start | bytes 2752516
  488.8 225.5 %reduce-scatter.11.cloned.1.call-start = ((), (), s32[]{:S(2)}) async-start(), calls=%async_computation.7 | async-start | bytes 974848 | tf_op jit(solution)/shard_map/reduce_scatter | solution.py:34
Sparse Core Ops, SparseCore 0:
  14.4 145.7 all-reduce.2
  163.0 69.2 reduce-scatter.4
  328.1 64.6 reduce-scatter.6
  488.9 64.6 reduce-scatter.8
  649.6 64.6 reduce-scatter.10
where the time goes:
time: 818 us; the launch traced here: 817 us
  waiting for transfers between devices  392 us (48%)
  blocking collectives  368 us (45%)
  between operations  29 us (4%)
  other arithmetic  14.8 us (2%)
  matrix products  9.26 us (1%)
    psum x4, blocking collectives, body(): sums = lax.psum(jnp.sum(shifted * shifted, axis=1), 'col')  251 us
    reduce_scatter x4, waiting for transfers between devices, body(): lax.psum_scatter(partial_grad, 'tok', scatter_dimension=0, tiled=True)  246 us
    psum x1, waiting for transfers between devices, from_root(): return lax.psum(block, axis)  146 us
    all_gather x4, blocking collectives, body(): change = lax.all_gather(local_change, 'tok', axis=0, tiled=True)  118 us
  transfers between devices with their start and end apart: 5, of which 5 were waited for; matrix products, arithmetic and copies ran while one was open for 1% of the time, Pallas kernels for 0%

commit v1 on v0

--- a/solution.py
+++ b/solution.py
@@ -38,7 +38,9 @@
         fresh = factor[:, None] * shifted
         local_change = (fresh - current).astype(jnp.bfloat16)
         state = lax.dynamic_update_index_in_dim(state, fresh, which, 0)
-        change = lax.all_gather(local_change, "tok", axis=0, tiled=True)
+        change = jnp.concatenate(
+            lax.all_to_all(jnp.stack([local_change] * lax.axis_size("tok")), "tok", 0, 0), axis=0
+        )
         resid = resid + jnp.dot(block_acts, change, preferred_element_type=jnp.float32) / scale
     return (state, resid)
 

time: 818 us -> 827 us (1.011)
  the two profiles are of different devices: /device:TPU:32 before, /device:TPU:96 now
where the time goes in v1:
time: 827 us; the launch traced here: 826 us
  waiting for transfers between devices  405 us (49%)
  blocking collectives  355 us (43%)
  between operations  28.8 us (3%)
  other arithmetic  14.8 us (2%)
  starting transfers between devices  9.51 us (1%)
  matrix products  9.25 us (1%)
    psum x4, blocking collectives, body(): sums = lax.psum(jnp.sum(shifted * shifted, axis=1), 'col')  251 us
    reduce_scatter x4, waiting for transfers between devices, body(): lax.psum_scatter(partial_grad, 'tok', scatter_dimension=0, tiled=True)  235 us
    psum x1, waiting for transfers between devices, from_root(): return lax.psum(block, axis)  145 us
    all_to_all x3, blocking collectives, body(): lax.all_to_all(jnp.stack([local_change] * lax.axis_size('tok')), 'tok', 0...  105 us
    all_to_all x1, waiting for transfers between devices, body(): lax.all_to_all(jnp.stack([local_change] * lax.axis_size('tok')), 'tok', 0...  25 us
  transfers between devices with their start and end apart: 6, of which 6 were waited for; matrix products, arithmetic and copies ran while one was open for 1% of the time, Pallas kernels for 0%

profile of v1, /device:TPU:96, one launch (start us, length us, event | category | flops | bytes accessed | tf_op | source)
XLA Modules:
  0.0 826.2 jit_solution(7199961685100313640)
XLA Ops:
  7.2 0.0 all-reduce.3.cloned.1.call-start
  7.2 1.4 fusion.18
  11.1 3.1 broadcast_select_fusion
  14.3 0.0 reduce-scatter.5.cloned.1.call-start
  14.3 145.1 %all-reduce.3.cloned.1.call-done = (bf16[512,896]{1,0:T(8,128)(2,1)}, bf16[512,896]{1,0:T(8,128)(2,1)}, bf16[512,896]{1,0:T(8,128)(2,1)}, bf16[512,896]{1,0:T(8,128)(2,1)}) async-done(((bf16[512,896]{1,0:T(8,128)(2,1)}, bf16[512,896]{1,0:T(8,128)(2,1)}, bf16[512,896]{1,0:T(8,128)(2,1)}, bf16[512,896]{1,0:T(8,128)(2,1)}), (bf16[512,896]{1,0:T(8,128)(2,1)}, bf16[512,896]{1,0:T(8,128)(2,1)}, ...) | async-done | bytes 3670032 | tf_op jit(solution)/shard_map/psum | solution.py:14
  159.4 2.5 fusion.10
  162.0 0.0 reduce-scatter.5.cloned.1.call-update
  162.0 0.0 reduce-scatter.7.cloned.1.call-start
  167.0 1.4 convert_element_type.27
  170.8 0.7 fusion.17
  172.1 0.7 fusion.16
  173.5 58.2 %reduce-scatter.5.cloned.1.call-done = f32[56,256]{1,0:T(8,128)} async-done(((f32[896,256]{1,0:T(8,128)}), f32[56,256]{1,0:T(8,128)}) %reduce-scatter.5.cloned.1.call-update) | async-done | bytes 57360 | tf_op jit(solution)/shard_map/reduce_scatter | solution.py:34
  231.7 1.0 multiply_reduce_fusion.3
  232.7 62.7 %psum.57 = f32[56]{0:T(128)S(1)} all-reduce(f32[56]{0:T(128)S(1)} %get-tuple-element.12), channel_id=1, replica_groups=mesh['tok'=16,'col'=32] {'col'}, use_global_device_ids=true, to_apply=%region_3.4 | all-reduce | flops 56 | bytes 448 | tf_op jit(solution)/shard_map/psum | solution.py:36
  295.3 0.9 fusion.15
  296.3 34.9 %all_to_all.20 = bf16[16,56,256]{2,1,0:T(8,128)(2,1)S(1)} all-to-all(bf16[16,56,256]{2,1,0:T(8,128)(2,1)S(1)} %stack.8), channel_id=1, replica_groups=mesh['tok'=16,'col'=32] {'tok'}, dimensions={0} | all-to-all | bytes 917504 | tf_op jit(solution)/shard_map/all_to_all | solution.py:42
  331.2 0.4 fusion
  331.7 1.4 fusion.8
  333.0 0.0 reduce-scatter.7.cloned.1.call-update
  333.1 0.0 reduce-scatter.9.cloned.1.call-start
  334.2 0.7 bitcast_dynamic-update-slice_fusion.3
  334.9 58.9 %reduce-scatter.7.cloned.1.call-done = f32[56,256]{1,0:T(8,128)} async-done(((f32[896,256]{1,0:T(8,128)}), f32[56,256]{1,0:T(8,128)}) %reduce-scatter.7.cloned.1.call-update) | async-done | bytes 57360 | tf_op jit(solution)/shard_map/reduce_scatter | solution.py:34
  393.8 1.0 multiply_reduce_fusion.2
  394.8 62.7 %psum.59 = f32[56]{0:T(128)S(1)} all-reduce(f32[56]{0:T(128)S(1)} %get-tuple-element.10), channel_id=1, replica_groups=mesh['tok'=16,'col'=32] {'col'}, use_global_device_ids=true, to_apply=%region_7.8 | all-reduce | flops 56 | bytes 448 | tf_op jit(solution)/shard_map/psum | solution.py:36
  457.5 0.9 fusion.14
  458.4 34.9 %all_to_all.21 = bf16[16,56,256]{2,1,0:T(8,128)(2,1)S(1)} all-to-all(bf16[16,56,256]{2,1,0:T(8,128)(2,1)S(1)} %stack.9), channel_id=1, replica_groups=mesh['tok'=16,'col'=32] {'tok'}, dimensions={0} | all-to-all | bytes 917504 | tf_op jit(solution)/shard_map/all_to_all | solution.py:42
  493.3 0.4 fusion.1
  493.8 1.4 fusion.6
  495.2 0.0 reduce-scatter.11.cloned.1.call-start
  496.6 0.7 bitcast_dynamic-update-slice_fusion.2
  497.3 58.7 %reduce-scatter.9.cloned.1.call-done = f32[56,256]{1,0:T(8,128)} async-done(((f32[896,256]{1,0:T(8,128)}), f32[56,256]{1,0:T(8,128)}) %reduce-scatter.9.cloned.1.call-update) | async-done | bytes 57360 | tf_op jit(solution)/shard_map/reduce_scatter | solution.py:34
  556.0 1.0 multiply_reduce_fusion.1
  557.0 62.7 %psum.61 = f32[56]{0:T(128)S(1)} all-reduce(f32[56]{0:T(128)S(1)} %get-tuple-element.8), channel_id=1, replica_groups=mesh['tok'=16,'col'=32] {'col'}, use_global_device_ids=true, to_apply=%region_11.12 | all-reduce | flops 56 | bytes 448 | tf_op jit(solution)/shard_map/psum | solution.py:36
  619.7 0.9 fusion.13
  620.6 34.9 %all_to_all.22 = bf16[16,56,256]{2,1,0:T(8,128)(2,1)S(1)} all-to-all(bf16[16,56,256]{2,1,0:T(8,128)(2,1)S(1)} %stack.10), channel_id=1, replica_groups=mesh['tok'=16,'col'=32] {'tok'}, dimensions={0} | all-to-all | bytes 917504 | tf_op jit(solution)/shard_map/all_to_all | solution.py:42
  655.5 0.4 fusion.2
  656.0 1.4 fusion.4
  657.4 0.0 reduce-scatter.11.cloned.1.call-update
  658.7 0.7 bitcast_dynamic-update-slice_fusion.1
  659.4 58.8 %reduce-scatter.11.cloned.1.call-done = f32[56,256]{1,0:T(8,128)} async-done(((f32[896,256]{1,0:T(8,128)}), f32[56,256]{1,0:T(8,128)}) %reduce-scatter.11.cloned.1.call-update) | async-done | bytes 57360 | tf_op jit(solution)/shard_map/reduce_scatter | solution.py:34
  718.2 1.0 multiply_reduce_fusion
  719.1 62.7 %psum.63 = f32[56]{0:T(128)S(1)} all-reduce(f32[56]{0:T(128)S(1)} %get-tuple-element.6), channel_id=1, replica_groups=mesh['tok'=16,'col'=32] {'col'}, use_global_device_ids=true, to_apply=%region_15.16 | all-reduce | flops 56 | bytes 448 | tf_op jit(solution)/shard_map/psum | solution.py:36
  781.8 0.9 fusion.12
  782.7 0.8 stack.11
  783.5 9.3 %all-to-all-start.3 = ((bf16[16,56,256]{2,1,0:T(8,128)(2,1)}), bf16[16,56,256]{2,1,0:T(8,128)(2,1)S(1)}, u32[]{:S(2)}, u32[]{:S(2)}) async-start(bf16[16,56,256]{2,1,0:T(8,128)(2,1)} %stack.11), calls=%async_computation.7 | async-start | bytes 917504 | tf_op jit(solution)/shard_map/all_to_all | solution.py:42
  792.8 0.7 bitcast_dynamic-update-slice_fusion
  793.5 25.0 %all-to-all-done.3 = bf16[16,56,256]{2,1,0:T(8,128)(2,1)S(1)} async-done(((bf16[16,56,256]{2,1,0:T(8,128)(2,1)}), bf16[16,56,256]{2,1,0:T(8,128)(2,1)S(1)}, u32[]{:S(2)}, u32[]{:S(2)}) %all-to-all-start.3) | async-done | bytes 458784 | tf_op jit(solution)/shard_map/all_to_all | solution.py:42
  818.5 1.2 fusion.3
  (25 shorter events, 0.2 us)
Async XLA Ops:
  7.2 152.3 %all-reduce.3.cloned.1.call-start = ((), (), s32[]{:S(2)}) async-start(), calls=%async_computation.12 | async-start | bytes 7340032 | tf_op jit(solution)/shard_map/psum | solution.py:14
  14.2 145.2 %copy-start.4 = (f32[512,256]{1,0:T(8,128)S(1)}, f32[512,256]{1,0:T(8,128)}, u32[]{:S(2)}) copy-start(f32[512,256]{1,0:T(8,128)} %param.7) | copy-start | bytes 1572868
  14.2 152.7 %copy-start.5 = (bf16[32,56,256]{2,1,0:T(8,128)(2,1)S(1)}, bf16[32,56,256]{2,1,0:T(8,128)(2,1)}, u32[]{:S(2)}) copy-start(bf16[32,56,256]{2,1,0:T(8,128)(2,1)} %param.8) | copy-start | bytes 2752516
  14.3 217.4 %reduce-scatter.5.cloned.1.call-start = ((), (), s32[]{:S(2)}) async-start(), calls=%async_computation.8 | async-start | bytes 974848 | tf_op jit(solution)/shard_map/reduce_scatter | solution.py:34
  162.0 8.8 %copy-start.6 = (f32[32]{0:T(128)S(1)}, f32[32]{0:T(128)}, u32[]{:S(2)}) copy-start(f32[32]{0:T(128)} %param.10) | copy-start | bytes 388
  162.0 10.1 %copy-start.7 = (f32[32]{0:T(128)S(1)}, f32[32]{0:T(128)}, u32[]{:S(2)}) copy-start(f32[32]{0:T(128)} %param.11) | copy-start | bytes 388
  162.0 231.8 %reduce-scatter.7.cloned.1.call-start = ((), (), s32[]{:S(2)}) async-start(), calls=%async_computation.9 | async-start | bytes 974848 | tf_op jit(solution)/shard_map/reduce_scatter | solution.py:34
  167.0 164.2 %copy-start.3 = (bf16[512,896]{1,0:T(8,128)(2,1)S(1)}, bf16[512,896]{1,0:T(8,128)(2,1)}, u32[]{:S(2)}) copy-start(bf16[512,896]{1,0:T(8,128)(2,1)} %get-tuple-element.2) | copy-start | bytes 2752516
  296.3 35.4 %copy-start.2 = (bf16[512,896]{1,0:T(8,128)(2,1)S(1)}, bf16[512,896]{1,0:T(8,128)(2,1)}, u32[]{:S(2)}) copy-start(bf16[512,896]{1,0:T(8,128)(2,1)} %get-tuple-element.3) | copy-start | bytes 2752516
  333.1 222.9 %reduce-scatter.9.cloned.1.call-start = ((), (), s32[]{:S(2)}) async-start(), calls=%async_computation.10 | async-start | bytes 974848 | tf_op jit(solution)/shard_map/reduce_scatter | solution.py:34
  458.4 35.4 %copy-start.1 = (bf16[512,896]{1,0:T(8,128)(2,1)S(1)}, bf16[512,896]{1,0:T(8,128)(2,1)}, u32[]{:S(2)}) copy-start(bf16[512,896]{1,0:T(8,128)(2,1)} %get-tuple-element.4) | copy-start | bytes 2752516
  495.2 222.9 %reduce-scatter.11.cloned.1.call-start = ((), (), s32[]{:S(2)}) async-start(), calls=%async_computation.11 | async-start | bytes 974848 | tf_op jit(solution)/shard_map/reduce_scatter | solution.py:34
  620.6 35.4 %copy-start = (bf16[512,896]{1,0:T(8,128)(2,1)S(1)}, bf16[512,896]{1,0:T(8,128)(2,1)}, u32[]{:S(2)}) copy-start(bf16[512,896]{1,0:T(8,128)(2,1)} %get-tuple-element.5) | copy-start | bytes 2752516
  783.5 35.0 %all-to-all-start.3 = ((bf16[16,56,256]{2,1,0:T(8,128)(2,1)}), bf16[16,56,256]{2,1,0:T(8,128)(2,1)S(1)}, u32[]{:S(2)}, u32[]{:S(2)}) async-start(bf16[16,56,256]{2,1,0:T(8,128)(2,1)} %stack.11), calls=%async_computation.7 | async-start | bytes 917504 | tf_op jit(solution)/shard_map/all_to_all | solution.py:42
Sparse Core Ops, SparseCore 0:
  14.4 145.0 all-reduce.2
  162.2 69.4 reduce-scatter.4
  333.2 60.5 reduce-scatter.6
  495.4 60.6 reduce-scatter.8
  657.5 60.6 reduce-scatter.10
